TPU v7x, 32 devices: a whole 2x2x4 slice. The times are simulated.
32 devices in a mesh: dp: 8 (over z, x), fsdp: 4 (over y, core).
Axes of the slice: x: 2, y: 2, z: 4, core: 2. Of those that a mesh axis runs over, the one named last changes fastest.
Arguments:
- inputs: bfloat16 [128, 14, 14, 256], P(('dp', 'fsdp')), may hold values from -6 to 6
- out_grads: bfloat16 [128, 14, 14, 256], P(('dp', 'fsdp')), may hold values from -6 to 6
- patch_basis: bfloat16 [1152, 2304], P(None, 'fsdp'), may hold values from -0.1875 to 0.1875
- output_basis: bfloat16 [256, 256], P(None, 'fsdp'), may hold values from -0.375 to 0.375
Outputs:
- second_moment: float32 [256, 2304], P('dp', 'fsdp')
- scaled_sum: float32 [256, 2304], P('dp', 'fsdp')
All inputs are finite; a program needn't handle non-finite values.
Results may differ from a plain program's by a relative error of at most 0.0041.
Values may be sent and summed in bfloat16 or wider, within the bound.
A program may use at most 64 MiB of HBM per device.

v0:
```python
import math

import jax
import jax.numpy as jnp
from jax import lax
from jax.sharding import PartitionSpec as P


def patch_rows(feature_maps):
    count = feature_maps.shape[0]
    grid_side = feature_maps.shape[1]
    padded = jnp.pad(feature_maps, ((0, 0), (1, 1), (1, 1), (0, 0)))
    shifted = [
        padded[:, row_tap : row_tap + grid_side, col_tap : col_tap + grid_side, :]
        for row_tap in range(3)
        for col_tap in range(3)
    ]
    return jnp.concatenate(shifted, axis=3).reshape(count, grid_side * grid_side, -1)


def on_device(inputs, out_grads, patch_basis, output_basis):
    examples_dev = inputs.shape[0]
    grid_side = inputs.shape[1]
    block_width = patch_basis.shape[0]
    out_width = output_basis.shape[0]
    total_examples = examples_dev * lax.axis_size("dp") * lax.axis_size("fsdp")
    inv_side = 1.0 / grid_side
    full_patch, full_out = (
        lax.all_gather(patch_basis, "fsdp", axis=1, tiled=True),
        lax.all_gather(output_basis, "fsdp", axis=1, tiled=True),
    )
    columns = full_patch.shape[1]

    def accumulate(position, running):
        example_input = lax.dynamic_index_in_dim(inputs, position, 0, keepdims=True)
        example_grad = lax.dynamic_index_in_dim(out_grads, position, 0, keepdims=False)
        patches = patch_rows(example_input)[0]
        low_part = jnp.dot(
            patches[:, :block_width],
            full_patch[:, :block_width],
            preferred_element_type=jnp.float32,
        )
        high_part = jnp.dot(
            patches[:, block_width:],
            full_patch[:, block_width:],
            preferred_element_type=jnp.float32,
        )
        rotated = jnp.concatenate([low_part, high_part], axis=1).astype(jnp.bfloat16)
        grad_rot = jnp.dot(
            example_grad.reshape(-1, out_width), full_out, preferred_element_type=jnp.float32
        ).astype(jnp.bfloat16)
        projected = jnp.dot(grad_rot.T, rotated, preferred_element_type=jnp.float32) * inv_side
        return (running[0] + projected * projected, running[1] + projected)

    empty_sums = jnp.zeros((out_width, columns), jnp.float32)
    squares, linear = lax.fori_loop(0, examples_dev, accumulate, (empty_sums, empty_sums))
    squares, linear = (
        lax.psum_scatter(squares, "fsdp", scatter_dimension=1, tiled=True),
        lax.psum_scatter(linear, "fsdp", scatter_dimension=1, tiled=True),
    )
    squares, linear = (
        lax.psum_scatter(squares, "dp", scatter_dimension=0, tiled=True),
        lax.psum_scatter(linear, "dp", scatter_dimension=0, tiled=True),
    )
    return (squares / total_examples, linear * (1.0 / math.sqrt(total_examples)))


def solution(mesh):
    in_specs = (
        P(("dp", "fsdp"), None, None, None),
        P(("dp", "fsdp"), None, None, None),
        P(None, "fsdp"),
        P(None, "fsdp"),
    )
    out_specs = (P("dp", "fsdp"), P("dp", "fsdp"))
    return jax.shard_map(
        on_device, mesh=mesh, in_specs=in_specs, out_specs=out_specs, check_vma=False
    )
```

profile of v0, /device:TPU:11, one launch (start us, length us, event | category | flops | bytes accessed | tf_op | source)
XLA Modules:
  0.0 319.0 jit_solution(17858851756259946846)
XLA Ops:
  8.0 6.1 %all_gather.6 = bf16[256,256]{0,1:T(8,128)(2,1)S(1)} all-gather(bf16[256,64]{0,1:T(8,128)(2,1)} %param.9), channel_id=1, replica_groups=mesh['dp'=8,'fsdp'=4] {'fsdp'}, dimensions={1}, use_global_device_ids=true | all-gather | bytes 163840 | tf_op jit(solution)/shard_map/all_gather | solution.py:30
  17.6 34.4 %all-gather.2.cloned.1.call-done = bf16[1152,2304]{0,1:T(8,128)(2,1)} async-done(((bf16[1152,576]{0,1:T(8,128)(2,1)}), bf16[1152,2304]{0,1:T(8,128)(2,1)}) %all-gather.2.cloned.1.call-update) | async-done | bytes 5308432 | tf_op jit(solution)/shard_map/all_gather | solution.py:29
  52.0 8.5 %copy.15 = bf16[1152,2304]{1,0:T(8,128)(2,1)} copy(bf16[1152,2304]{0,1:T(8,128)(2,1)} %all-gather.2.cloned.1.call-done) | data formatting | bytes 10616832
  60.5 52.0 %while.18 = (s32[]{:T(128)}, f32[256,2304]{1,0:T(8,128)}, f32[256,2304]{1,0:T(8,128)S(1)}, bf16[4,14,14,256]{3,2,1,0:T(8,128)(2,1)}, bf16[256,256]{1,0:T(8,128)(...) while((s32[]{:T(128)}, f32[256,2304]{1,0:T(8,128)}, ...), condition=%wide.region_1.2_spmd.clone, body=%wide.region_0.1_spmd.clone.sunk | while | flops 1303197696 | bytes 26702024 | solution.py:56
  63.7 2.8 fusion.33
  66.5 2.6 fusion.32
  69.2 3.1 select_add_fusion.3
  75.5 2.8 fusion.33
  78.3 2.6 fusion.32
  80.9 4.8 %select_add_fusion.3 = (f32[256,2304]{1,0:T(8,128)S(1)}, f32[256,2304]{1,0:T(8,128)}) fusion(f32[256,2304]{1,0:T(8,128)S(1)} %get-tuple-element.299, pred[]{:T(512)S(6)} %compare.4, f32[256,2304]{1,0:T(8,128)} %get-tuple-element.298, bf16[196,1152]{1,0:T(8,128)(2,1)S(1)} %fusion.32, bf16[196,1152]{1,0:T(8,128)(2,1)S(1)} %fusion.33, ...), kind=kOutput, calls=%fused_computation.7.clone.1 | convolution fusion | flops 262296576 | bytes 10571777 | tf_op jit(solution)/shard_map/while/body/eval_jaxpr/dot_general | solution.py:52
  88.9 2.8 fusion.33
  91.7 2.6 fusion.32
  94.4 4.8 %select_add_fusion.3 = (f32[256,2304]{1,0:T(8,128)S(1)}, f32[256,2304]{1,0:T(8,128)}) fusion(f32[256,2304]{1,0:T(8,128)S(1)} %get-tuple-element.299, pred[]{:T(512)S(6)} %compare.4, f32[256,2304]{1,0:T(8,128)} %get-tuple-element.298, bf16[196,1152]{1,0:T(8,128)(2,1)S(1)} %fusion.32, bf16[196,1152]{1,0:T(8,128)(2,1)S(1)} %fusion.33, ...), kind=kOutput, calls=%fused_computation.7.clone.1 | convolution fusion | flops 262296576 | bytes 10571777 | tf_op jit(solution)/shard_map/while/body/eval_jaxpr/dot_general | solution.py:52
  102.3 2.8 fusion.33
  105.1 2.6 fusion.32
  107.8 4.8 %select_add_fusion.3 = (f32[256,2304]{1,0:T(8,128)S(1)}, f32[256,2304]{1,0:T(8,128)}) fusion(f32[256,2304]{1,0:T(8,128)S(1)} %get-tuple-element.299, pred[]{:T(512)S(6)} %compare.4, f32[256,2304]{1,0:T(8,128)} %get-tuple-element.298, bf16[196,1152]{1,0:T(8,128)(2,1)S(1)} %fusion.32, bf16[196,1152]{1,0:T(8,128)(2,1)S(1)} %fusion.33, ...), kind=kOutput, calls=%fused_computation.7.clone.1 | convolution fusion | flops 262296576 | bytes 10571777 | tf_op jit(solution)/shard_map/while/body/eval_jaxpr/dot_general | solution.py:52
  112.6 2.0 copy.18
  116.2 1.9 copy.16
  118.2 29.1 %reduce-scatter.15.cloned.1.call-done = f32[576,256]{1,0:T(8,128)} async-done(((f32[2304,256]{1,0:T(8,128)}), f32[576,256]{1,0:T(8,128)}) %reduce-scatter.15.cloned.1.call-update) | async-done | bytes 589840
  147.3 2.1 copy.19
  149.5 33.6 %reduce-scatter.13.cloned.1.call-done = f32[576,256]{1,0:T(8,128)} async-done(((f32[2304,256]{1,0:T(8,128)}), f32[576,256]{1,0:T(8,128)}) %reduce-scatter.13.cloned.1.call-update) | async-done | bytes 589840
  183.1 2.1 copy.17
  185.3 61.0 %reduce-scatter.11.cloned.1.call-done = f32[32,576]{1,0:T(8,128)} async-done(((f32[256,576]{1,0:T(8,128)}), f32[32,576]{1,0:T(8,128)}) %reduce-scatter.11.cloned.1.call-update) | async-done | bytes 73744 | tf_op jit(solution)/shard_map/reduce_scatter | solution.py:63
  247.8 63.1 %reduce-scatter.9.cloned.1.call-done = f32[32,576]{1,0:T(8,128)} async-done(((f32[256,576]{1,0:T(8,128)}), f32[32,576]{1,0:T(8,128)}) %reduce-scatter.9.cloned.1.call-update) | async-done | bytes 73744 | tf_op jit(solution)/shard_map/reduce_scatter | solution.py:62
  (93 shorter events, 21.5 us)
Async XLA Ops:
  7.2 9.6 %copy-start.4 = (bf16[4,14,14,256]{3,0,2,1:T(4,128)(2,1)S(1)}, bf16[4,14,14,256]{3,0,2,1:T(4,128)(2,1)}, u32[]{:S(2)}) copy-start(bf16[4,14,14,256]{3,0,2,1:T(4,128)(2,1)} %param.7) | copy-start | bytes 1204228
  7.2 44.8 %all-gather.2.cloned.1.call-start = ((), (), s32[]{:S(2)}) async-start(), calls=%async_computation.4 | async-start | bytes 6635520 | tf_op jit(solution)/shard_map/all_gather | solution.py:29
  7.9 139.4 %reduce-scatter.15.cloned.1.call-start = ((), (), s32[]{:S(2)}) async-start(), calls=%async_computation.8 | async-start | bytes 2949120
  63.7 2.8 copy-start.1
  66.5 2.7 copy-start.2
  66.5 2.7 copy-start.3
  75.5 2.8 copy-start.1
  78.3 2.7 copy-start.2
  78.3 2.7 copy-start.3
  88.9 2.8 copy-start.1
  91.7 2.7 copy-start.2
  91.7 2.7 copy-start.3
  102.3 2.8 copy-start.1
  105.1 2.7 copy-start.2
  105.1 2.7 copy-start.3
  114.5 1.7 copy-start
  114.5 68.6 %reduce-scatter.13.cloned.1.call-start = ((), (), s32[]{:S(2)}) async-start(), calls=%async_computation.7 | async-start | bytes 2949120
  118.1 128.2 %reduce-scatter.11.cloned.1.call-start = ((), (), s32[]{:S(2)}) async-start(), calls=%async_computation.6 | async-start | bytes 737280 | tf_op jit(solution)/shard_map/reduce_scatter | solution.py:63
  149.5 161.4 %reduce-scatter.9.cloned.1.call-start = ((), (), s32[]{:S(2)}) async-start(), calls=%async_computation.5 | async-start | bytes 737280 | tf_op jit(solution)/shard_map/reduce_scatter | solution.py:62
Sparse Core Ops, SparseCore 0:
  9.6 42.3 all-gather.1
  114.7 32.6 reduce-scatter.14
  150.0 33.0 reduce-scatter.12
  186.2 60.0 reduce-scatter.10
  249.8 61.0 reduce-scatter.8
where the time goes:
time: 323 us; the launch traced here: 319 us
  waiting for transfers between devices  222 us (69%)
  matrix products  39.1 us (12%)
  local copies, waits for them, and re-layouts  34.3 us (11%)
  between operations  13.8 us (4%)
  blocking collectives  6.15 us (2%)
    unnamed x7, waiting for transfers between devices  63.4 us
    reduce_scatter x1, waiting for transfers between devices, on_device(): lax.psum_scatter(squares, 'dp', scatter_dimension=0, tiled=True)  63.1 us
    reduce_scatter x1, waiting for transfers between devices, on_device(): lax.psum_scatter(linear, 'dp', scatter_dimension=0, tiled=True)  61 us
    all_gather x1, waiting for transfers between devices, on_device(): lax.all_gather(patch_basis, 'fsdp', axis=1, tiled=True)  34.4 us
    unnamed x12, local copies, waits for them, and re-layouts  21.8 us
    dot_general x4, matrix products, accumulate(): jnp.dot(grad_rot.T, rotated, preferred_element_type=jnp.float32) * inv_side  17.4 us
    dot_general x4, matrix products, accumulate(): jnp.dot(patches[:, :block_width], full_patch[:, :block_width], preferred_...  11.2 us
    dot_general x4, matrix products, accumulate(): jnp.dot(patches[:, block_width:], full_patch[:, block_width:], preferred_...  10.5 us
  transfers between devices with their start and end apart: 5, of which 5 were waited for; matrix products, arithmetic and copies ran while one was open for 4% of the time, Pallas kernels for 0%

commit v1 on v0

v1 whole, which is shorter than its diff:
```python
import functools
import math

import jax
import jax.numpy as jnp
from jax import lax
from jax.experimental import pallas as pl
from jax.experimental.pallas import tpu as pltpu
from jax.sharding import PartitionSpec as P

MESH = pl.DeviceIdType.MESH
HALVES = 2
PADDED = 16
LANES = 128


def kernel(
    nd, nf, examples, x_ref, g_ref, pb_ref, ob_ref, sq_out, ln_out,
    xbuf, gstage, obbuf, rot, gr, taps, shifts, sq, ln, rs_send, rs_recv,
    ob_snd, ob_rcv, x_snd, x_rcv, g_snd, g_rcv, r_snd, r_rcv,
):
    d = lax.axis_index("dp")
    f = lax.axis_index("fsdp")
    nh = nf // 2
    h, c = f // 2, f % 2
    sibling = 2 * h + 1 - c
    side = x_ref.shape[1]
    channels = x_ref.shape[3]
    height, cols = pb_ref.shape
    outc = ob_ref.shape[0]
    own_cols = ob_ref.shape[1]
    rows = side * PADDED
    flat = xbuf.shape[1] * PADDED
    quart = outc // HALVES
    per_dp = quart // nd
    total = nd * nf * examples
    f32, bf16 = jnp.float32, jnp.bfloat16

    barrier = pltpu.get_barrier_semaphore()
    pl.semaphore_signal(barrier, inc=1, device_id=(d, sibling), device_id_type=MESH)
    for j in range(1, nh):
        pl.semaphore_signal(
            barrier, inc=1, device_id=(d, 2 * ((h + j) % nh) + c), device_id_type=MESH
        )
    for j in range(1, nd):
        pl.semaphore_signal(barrier, inc=1, device_id=((d + j) % nd, f), device_id_type=MESH)

    def source(j, t):
        return 2 * ((h + j) % nh) + c + t * (1 - 2 * c)

    def clear(n, carry):
        xbuf[n, 0] = jnp.zeros((PADDED, channels), bf16)
        xbuf[n, pl.ds(side + 1, xbuf.shape[1] - side - 1)] = jnp.zeros(
            (xbuf.shape[1] - side - 1, PADDED, channels), bf16
        )
        return carry

    lax.fori_loop(0, nf * examples, clear, 0)

    def stage(e, carry):
        n = f * examples + e
        xbuf[n, pl.ds(1, side)] = jnp.zeros((side, PADDED, channels), bf16)
        xbuf[n, pl.ds(1, side), pl.ds(0, side), :] = x_ref[e]
        gstage[e] = jnp.zeros((side, PADDED, outc), bf16)
        gstage[e, :, pl.ds(0, side), :] = g_ref[e]
        return carry

    lax.fori_loop(0, examples, stage, 0)
    obbuf[f] = ob_ref[...]

    pl.semaphore_wait(barrier, nd - 1 + nh)

    def route(j, t):
        to = jnp.where(t == 1, sibling, 2 * ((h + j) % nh) + c)
        back = (nh - j) % nh if isinstance(j, int) else lax.rem(nh - j, nh)
        return (d, to), back

    def ob_copy(j, t, own):
        to, back = route(j, t)
        s = f if own else source(j, 0)
        slot = back if t == 0 else j
        return pltpu.make_async_remote_copy(
            src_ref=obbuf.at[s], dst_ref=obbuf.at[s], send_sem=ob_snd.at[j, t],
            recv_sem=ob_rcv.at[slot, t], device_id=to, device_id_type=MESH)

    def ob_arrival(j, t):
        s = source(j, t)
        return pltpu.make_async_remote_copy(
            src_ref=obbuf.at[s], dst_ref=obbuf.at[s], send_sem=ob_snd.at[j, t],
            recv_sem=ob_rcv.at[j, t], device_id=(d, sibling), device_id_type=MESH)

    def x_copy(j, t, e, own):
        to, back = route(j, t)
        s = f if own else source(j, 0)
        slot = back if t == 0 else j
        ref = xbuf.at[s * examples + e, pl.ds(1, side)]
        return pltpu.make_async_remote_copy(
            src_ref=ref, dst_ref=ref, send_sem=x_snd.at[j, t, e],
            recv_sem=x_rcv.at[slot, t, e], device_id=to, device_id_type=MESH)

    def x_arrival(j, t, e):
        ref = xbuf.at[source(j, t) * examples + e, pl.ds(1, side)]
        return pltpu.make_async_remote_copy(
            src_ref=ref, dst_ref=ref, send_sem=x_snd.at[j, t, e],
            recv_sem=x_rcv.at[j, t, e], device_id=(d, sibling), device_id_type=MESH)

    def g_copy(q, j, t, e, own):
        to, back = route(j, t)
        s = f if own else source(j, 0)
        slot = back if t == 0 else j
        ref = gr.at[q, s * examples + e]
        return pltpu.make_async_remote_copy(
            src_ref=ref, dst_ref=ref, send_sem=g_snd.at[q, j, t, e],
            recv_sem=g_rcv.at[q, slot, t, e], device_id=to, device_id_type=MESH)

    def g_arrival(q, j, t, e):
        ref = gr.at[q, source(j, t) * examples + e]
        return pltpu.make_async_remote_copy(
            src_ref=ref, dst_ref=ref, send_sem=g_snd.at[q, j, t, e],
            recv_sem=g_rcv.at[q, j, t, e], device_id=(d, sibling), device_id_type=MESH)

    def r_copy(q, j):
        return pltpu.make_async_remote_copy(
            src_ref=rs_send.at[q, j], dst_ref=rs_recv.at[q, j], send_sem=r_snd.at[q, j],
            recv_sem=r_rcv.at[q, j], device_id=((d + j) % nd, f), device_id_type=MESH)

    def each(count, body):
        def step(i, carry):
            body(i)
            return carry
        lax.fori_loop(0, count, step, 0)

    for j in range(1, nh):
        ob_copy(j, 0, True).start()
    ob_copy(0, 1, True).start()
    for j in range(1, nh):
        each(examples, lambda e: x_copy(j, 0, e, True).start())
    each(examples, lambda e: x_copy(0, 1, e, True).start())

    sq[...] = jnp.zeros_like(sq)
    ln[...] = jnp.zeros_like(ln)
    into = lax.broadcasted_iota(jnp.int32, (flat, flat), 0)
    out_of = lax.broadcasted_iota(jnp.int32, (flat, flat), 1)
    shifts[0] = (out_of == into - 1).astype(f32).astype(bf16)
    shifts[1] = (out_of == into + 1).astype(f32).astype(bf16)

    chunks = channels // LANES
    first = ((f * cols) // height) * (height // LANES)

    def rotate(n):
        plain = xbuf[n].reshape(flat, channels)
        before = jnp.dot(shifts[0], plain, preferred_element_type=f32).astype(bf16)
        after = jnp.dot(shifts[1], plain, preferred_element_type=f32).astype(bf16)
        for kx, value in enumerate((before, plain, after)):
            for k in range(chunks):
                taps[kx * chunks + k] = value[:, k * LANES : (k + 1) * LANES]
        pieces = []
        for i in range(height // LANES):
            at = first + i
            tap, k = at // chunks, at % chunks
            ky, kx = tap // 3, tap % 3
            start = pl.multiple_of(ky * PADDED, PADDED)
            pieces.append(taps[kx * chunks + k, pl.ds(start, rows), :])
        patches = jnp.concatenate(pieces, axis=1)
        rot[n] = jnp.dot(patches, pb_ref[...], preferred_element_type=f32).astype(bf16)

    def project(q, n):
        value = lax.dot_general(
            gr[q, n], rot[n], (((0,), (0,)), ((), ())), preferred_element_type=f32
        ) * (1.0 / side)
        sq[q] += value * value
        ln[q] += value

    each(examples, lambda e: rotate(f * examples + e))

    ob_arrival(0, 1).wait_recv()
    for j in range(1, nh):
        ob_arrival(j, 0).wait_recv()
        ob_copy(j, 1, False).start()
    for j in range(1, nh):
        ob_arrival(j, 1).wait_recv()
    column = lax.broadcasted_iota(jnp.int32, (own_cols, outc), 0)
    place = lax.broadcasted_iota(jnp.int32, (own_cols, outc), 1)
    half, rest = place // quart, place % quart
    wanted = (rest // per_dp) * (per_dp * HALVES) + half * per_dp + rest % per_dp
    basis = jnp.zeros((outc, outc), f32)
    for s in range(nf):
        pick = (column + s * own_cols == wanted).astype(f32).astype(bf16)
        basis = basis + jnp.dot(obbuf[s], pick, preferred_element_type=f32)
    basis = basis.astype(bf16)
    for e in range(examples):
        value = jnp.dot(
            gstage[e].reshape(rows, outc), basis, preferred_element_type=f32
        ).astype(bf16)
        for q in range(HALVES):
            gr[q, f * examples + e] = value[:, q * quart : (q + 1) * quart]
    for q in range(HALVES):
        for j in range(1, nh):
            each(examples, lambda e: g_copy(q, j, 0, e, True).start())
        each(examples, lambda e: g_copy(q, 0, 1, e, True).start())

    def own_project(e):
        for q in range(HALVES):
            project(q, f * examples + e)

    each(examples, own_project)

    def sibling_rotate(e):
        x_arrival(0, 1, e).wait_recv()
        rotate(sibling * examples + e)

    each(examples, sibling_rotate)

    def sibling_project(e):
        for q in range(HALVES):
            g_arrival(q, 0, 1, e).wait_recv()
            project(q, sibling * examples + e)

    each(examples, sibling_project)

    def far_rotate(i):
        j, e = 1 + i // examples, i % examples
        x_arrival(j, 0, e).wait_recv()
        x_copy(j, 1, e, False).start()
        rotate(source(j, 0) * examples + e)
        x_arrival(j, 1, e).wait_recv()
        rotate(source(j, 1) * examples + e)

    each((nh - 1) * examples, far_rotate)

    for q in range(HALVES):
        def far_project(i):
            j, e = 1 + i // examples, i % examples
            g_arrival(q, j, 0, e).wait_recv()
            g_copy(q, j, 1, e, False).start()
            project(q, source(j, 0) * examples + e)
            g_arrival(q, j, 1, e).wait_recv()
            project(q, source(j, 1) * examples + e)

        each((nh - 1) * examples, far_project)

        def hand_out(i):
            j = i + 1
            start = pl.multiple_of(((d + j) % nd) * per_dp, per_dp)
            both = jnp.concatenate(
                [sq[q, pl.ds(start, per_dp), :], ln[q, pl.ds(start, per_dp), :]], axis=0
            )
            rs_send[q, j] = both.astype(bf16)
            r_copy(q, j).start()

        each(nd - 1, hand_out)

    for q in range(HALVES):
        start = pl.multiple_of(d * per_dp, per_dp)
        total_sq = sq[q, pl.ds(start, per_dp), :]
        total_ln = ln[q, pl.ds(start, per_dp), :]
        for j in range(1, nd):
            r_copy(q, j).wait_recv()
            got = rs_recv[q, j].astype(f32)
            total_sq = total_sq + got[:per_dp]
            total_ln = total_ln + got[per_dp:]
        sq_out[pl.ds(q * per_dp, per_dp), :] = total_sq * (1.0 / total)
        ln_out[pl.ds(q * per_dp, per_dp), :] = total_ln * (1.0 / math.sqrt(total))

    ob_copy(0, 1, True).wait_send()
    each(examples, lambda e: x_copy(0, 1, e, True).wait_send())
    for q in range(HALVES):
        each(examples, lambda e: g_copy(q, 0, 1, e, True).wait_send())
        each(nd - 1, lambda i: r_copy(q, i + 1).wait_send())
    for j in range(1, nh):
        ob_copy(j, 0, True).wait_send()
        ob_copy(j, 1, False).wait_send()

        def sent(e):
            x_copy(j, 0, e, True).wait_send()
            x_copy(j, 1, e, False).wait_send()
            for q in range(HALVES):
                g_copy(q, j, 0, e, True).wait_send()
                g_copy(q, j, 1, e, False).wait_send()

        each(examples, sent)


def on_device(inputs, out_grads, patch_basis, output_basis):
    nd, nf = lax.axis_size("dp"), lax.axis_size("fsdp")
    nh = nf // 2
    examples, side, _, channels = inputs.shape
    cols = patch_basis.shape[1]
    outc, own_cols = output_basis.shape
    rows = side * PADDED
    quart = outc // HALVES
    per_dp = quart // nd
    held = nf * examples
    bf16, f32 = jnp.bfloat16, jnp.float32
    dma = pltpu.SemaphoreType.DMA
    vmem = pl.BlockSpec(memory_space=pltpu.VMEM)
    out = jax.ShapeDtypeStruct((outc // nd, cols), f32)
    return pl.pallas_call(
        functools.partial(kernel, nd, nf, examples),
        out_shape=(out, out),
        in_specs=[vmem] * 4,
        out_specs=(vmem, vmem),
        scratch_shapes=[
            pltpu.VMEM((held, side + 2, PADDED, channels), bf16),
            pltpu.VMEM((examples, side, PADDED, outc), bf16),
            pltpu.VMEM((nf, outc, own_cols), bf16),
            pltpu.VMEM((held, rows, cols), bf16),
            pltpu.VMEM((HALVES, held, rows, quart), bf16),
            pltpu.VMEM((3 * (channels // LANES), (side + 2) * PADDED, LANES), bf16),
            pltpu.VMEM((2, (side + 2) * PADDED, (side + 2) * PADDED), bf16),
            pltpu.VMEM((HALVES, quart, cols), f32),
            pltpu.VMEM((HALVES, quart, cols), f32),
            pltpu.VMEM((HALVES, nd, 2 * per_dp, cols), bf16),
            pltpu.VMEM((HALVES, nd, 2 * per_dp, cols), bf16),
            dma((nh, 2)),
            dma((nh, 2)),
            dma((nh, 2, examples)),
            dma((nh, 2, examples)),
            dma((HALVES, nh, 2, examples)),
            dma((HALVES, nh, 2, examples)),
            dma((HALVES, nd)),
            dma((HALVES, nd)),
        ],
        compiler_params=pltpu.CompilerParams(
            collective_id=0, has_side_effects=True, vmem_limit_bytes=52 * 1024 * 1024
        ),
    )(inputs, out_grads, patch_basis, output_basis)


def solution(mesh):
    in_specs = (
        P(("dp", "fsdp"), None, None, None),
        P(("dp", "fsdp"), None, None, None),
        P(None, "fsdp"),
        P(None, "fsdp"),
    )
    out_specs = (P("dp", "fsdp"), P("dp", "fsdp"))
    return jax.shard_map(
        on_device, mesh=mesh, in_specs=in_specs, out_specs=out_specs, check_vma=False
    )
```

time: 323 us -> 54.8 us (0.17); the launches traced: 319 us -> 54.6 us
  waiting for transfers between devices: 222 us -> 0 us
  Pallas kernels: 0 us -> 47.9 us
  matrix products: 39.1 us -> 0 us
  local copies, waits for them, and re-layouts: 34.3 us -> 6.04 us
  between operations: 13.8 us -> 0.67 us
  blocking collectives: 6.15 us -> 0 us
    reduce_scatter x2 -> x0, waiting for transfers between devices: 124 us -> none  [the longest x1 63.1 us: on_device(): lax.psum_scatter(squares, 'dp', scatter_dimension=0, tiled=True)]
    unnamed x7 -> x0, waiting for transfers between devices: 63.4 us -> none
    pallas_call x0 -> x1, Pallas kernels: none -> 47.9 us  [on_device(): pl.pallas_call(functools.partial(kernel, nd, nf, examples), out_shape=(ou...]
    dot_general x12 -> x0, matrix products: 39.1 us -> none  [the longest x4 17.4 us: accumulate(): jnp.dot(grad_rot.T, rotated, preferred_element_type=jnp.float32) * inv_side]
    all_gather x1 -> x0, waiting for transfers between devices: 34.4 us -> none  [on_device(): lax.all_gather(patch_basis, 'fsdp', axis=1, tiled=True)]
    unnamed x12 -> x8, local copies, waits for them, and re-layouts: 21.8 us -> 6.04 us
    reshape x8 -> x0, local copies, waits for them, and re-layouts: 7.56 us -> none  [the longest x4 4.83 us: accumulate(): patches = patch_rows(example_input)[0]]
    all_gather x1 -> x0, blocking collectives: 6.15 us -> none  [on_device(): lax.all_gather(output_basis, 'fsdp', axis=1, tiled=True)]
  transfers between devices with their start and end apart: 5 -> 0, of which waited for: 5 -> 0; matrix products, arithmetic and copies ran while one was open for 4% -> 0% of each run, Pallas kernels for 0% -> 0%
where the time goes in v1:
time: 54.8 us; the launch traced here: 54.6 us
  Pallas kernels  47.9 us (87%)
  local copies, waits for them, and re-layouts  6.04 us (11%)
  between operations  0.67 us (1%)
    pallas_call x1, Pallas kernels, on_device(): pl.pallas_call(functools.partial(kernel, nd, nf, examples), out_shape=(ou...  47.9 us
    unnamed x8, local copies, waits for them, and re-layouts  6.04 us

profile of v1, /device:TPU:11, one launch (start us, length us, event | category | flops | bytes accessed | tf_op | source)
XLA Modules:
  0.0 54.6 jit_solution(3766578715213991343)
XLA Ops:
  0.6 0.0 copy-start
  0.6 1.0 %copy.9.ob_ref = bf16[256,64]{1,0:T(8,128)(2,1)S(1)} copy(bf16[256,64]{0,1:T(8,128)(2,1)} %param.7) | data formatting | bytes 65536 | tf_op args[3]
  1.6 1.1 %copy.6.x_ref = bf16[4,14,14,256]{3,2,1,0:T(8,128)(2,1)S(1)} copy(bf16[4,14,14,256]{3,0,2,1:T(4,128)(2,1)} %param.4) | data formatting | bytes 802816 | tf_op args[0]
  2.7 1.1 %copy.7.g_ref = bf16[4,14,14,256]{3,2,1,0:T(8,128)(2,1)S(1)} copy(bf16[4,14,14,256]{3,0,2,1:T(4,128)(2,1)} %param.5) | data formatting | bytes 802816 | tf_op args[1]
  3.8 0.0 copy-done
  3.8 1.7 %copy.8.pb_ref = bf16[1152,576]{1,0:T(8,128)(2,1)} copy(bf16[1152,576]{0,1:T(8,128)(2,1)S(1)} %copy-done) | data formatting | bytes 2654208 | tf_op args[2]
  5.4 47.9 %shard_map.59 = (f32[32,576]{1,0:T(8,128)S(1)}, f32[32,576]{1,0:T(8,128)S(1)}) custom-call(bf16[4,14,14,256]{3,2,1,0:T(8,128)(2,1)S(1)} %copy.6.x_ref, bf16[4,14,14,256]{3,2,1,0:T(8,128)(2,1)S(1)} %copy.7.g_ref, bf16[1152,576]{1,0:T(8,128)(2,1)} %copy.8.pb_ref, bf16[256,64]{1,0:T(8,128)(2,1)S(1)} %copy.9.ob_ref), custom_call_target="tpu_custom_call" | custom-call | tf_op jit(solution)/shard_map/pallas_call | solution.py:298
  53.3 0.6 %copy.12 = f32[32,576]{1,0:T(8,128)} copy(f32[32,576]{1,0:T(8,128)S(1)} %get-tuple-element.4) | data formatting | bytes 147456
  53.9 0.6 %copy.13 = f32[32,576]{1,0:T(8,128)} copy(f32[32,576]{1,0:T(8,128)S(1)} %get-tuple-element.5) | data formatting | bytes 147456
Async XLA Ops:
  0.6 3.1 %copy-start = (bf16[1152,576]{0,1:T(8,128)(2,1)S(1)}, bf16[1152,576]{0,1:T(8,128)(2,1)}, u32[]{:S(2)}) copy-start(bf16[1152,576]{0,1:T(8,128)(2,1)} %param.6) | copy-start | bytes 3981316

commit v2 on v1

--- a/solution.py
+++ b/solution.py
@@ -15,7 +15,8 @@
 
 
 def kernel(
-    nd, nf, examples, x_ref, g_ref, pb_ref, ob_ref, sq_out, ln_out,
+    nd, nf, examples, x_hbm, g_hbm, pb_hbm, ob_hbm, sq_out, ln_out,
+    x_ref, g_ref, pb_ref, ob_ref, local,
     xbuf, gstage, obbuf, rot, gr, taps, shifts, sq, ln, rs_send, rs_recv,
     ob_snd, ob_rcv, x_snd, x_rcv, g_snd, g_rcv, r_snd, r_rcv,
 ):
@@ -48,6 +49,15 @@
     def source(j, t):
         return 2 * ((h + j) % nh) + c + t * (1 - 2 * c)
 
+    loads = [
+        pltpu.make_async_copy(src, dst, local.at[k])
+        for k, (src, dst) in enumerate(
+            ((x_hbm, x_ref), (ob_hbm, ob_ref), (g_hbm, g_ref), (pb_hbm, pb_ref))
+        )
+    ]
+    for load in loads:
+        load.start()
+
     def clear(n, carry):
         xbuf[n, 0] = jnp.zeros((PADDED, channels), bf16)
         xbuf[n, pl.ds(side + 1, xbuf.shape[1] - side - 1)] = jnp.zeros(
@@ -61,11 +71,11 @@
         n = f * examples + e
         xbuf[n, pl.ds(1, side)] = jnp.zeros((side, PADDED, channels), bf16)
         xbuf[n, pl.ds(1, side), pl.ds(0, side), :] = x_ref[e]
-        gstage[e] = jnp.zeros((side, PADDED, outc), bf16)
-        gstage[e, :, pl.ds(0, side), :] = g_ref[e]
         return carry
 
+    loads[0].wait()
     lax.fori_loop(0, examples, stage, 0)
+    loads[1].wait()
     obbuf[f] = ob_ref[...]
 
     pl.semaphore_wait(barrier, nd - 1 + nh)
@@ -147,22 +157,38 @@
     chunks = channels // LANES
     first = ((f * cols) // height) * (height // LANES)
 
-    def rotate(n):
-        plain = xbuf[n].reshape(flat, channels)
-        before = jnp.dot(shifts[0], plain, preferred_element_type=f32).astype(bf16)
-        after = jnp.dot(shifts[1], plain, preferred_element_type=f32).astype(bf16)
-        for kx, value in enumerate((before, plain, after)):
-            for k in range(chunks):
-                taps[kx * chunks + k] = value[:, k * LANES : (k + 1) * LANES]
-        pieces = []
-        for i in range(height // LANES):
-            at = first + i
-            tap, k = at // chunks, at % chunks
-            ky, kx = tap // 3, tap % 3
-            start = pl.multiple_of(ky * PADDED, PADDED)
-            pieces.append(taps[kx * chunks + k, pl.ds(start, rows), :])
-        patches = jnp.concatenate(pieces, axis=1)
-        rot[n] = jnp.dot(patches, pb_ref[...], preferred_element_type=f32).astype(bf16)
+    def rotate(slots):
+        lines = []
+        for b, n in enumerate(slots):
+            plain = xbuf[n].reshape(flat, channels)
+            before = jnp.dot(shifts[0], plain, preferred_element_type=f32).astype(bf16)
+            after = jnp.dot(shifts[1], plain, preferred_element_type=f32).astype(bf16)
+            for kx, value in enumerate((before, plain, after)):
+                for k in range(chunks):
+                    taps[b, kx * chunks + k] = value[:, k * LANES : (k + 1) * LANES]
+        for b, n in enumerate(slots):
+            pieces = []
+            for i in range(height // LANES):
+                at = first + i
+                tap, k = at // chunks, at % chunks
+                ky, kx = tap // 3, tap % 3
+                start = pl.multiple_of(ky * PADDED, PADDED)
+                pieces.append(taps[b, kx * chunks + k, pl.ds(start, rows), :])
+            lines.append(jnp.concatenate(pieces, axis=1))
+        patches = jnp.concatenate(lines, axis=0)
+        value = jnp.dot(patches, pb_ref[...], preferred_element_type=f32).astype(bf16)
+        for b, n in enumerate(slots):
+            rot[n] = value[b * rows : (b + 1) * rows]
+
+    def project_whole(n):
+        both = jnp.concatenate([gr[q, n] for q in range(HALVES)], axis=1)
+        value = lax.dot_general(
+            both, rot[n], (((0,), (0,)), ((), ())), preferred_element_type=f32
+        ) * (1.0 / side)
+        for q in range(HALVES):
+            part = value[q * quart : (q + 1) * quart]
+            sq[q] += part * part
+            ln[q] += part
 
     def project(q, n):
         value = lax.dot_general(
@@ -171,7 +197,8 @@
         sq[q] += value * value
         ln[q] += value
 
-    each(examples, lambda e: rotate(f * examples + e))
+    loads[3].wait()
+    rotate([f * examples + e for e in range(examples)])
 
     ob_arrival(0, 1).wait_recv()
     for j in range(1, nh):
@@ -188,7 +215,10 @@
         pick = (column + s * own_cols == wanted).astype(f32).astype(bf16)
         basis = basis + jnp.dot(obbuf[s], pick, preferred_element_type=f32)
     basis = basis.astype(bf16)
+    loads[2].wait()
     for e in range(examples):
+        gstage[e] = jnp.zeros((side, PADDED, outc), bf16)
+        gstage[e, :, pl.ds(0, side), :] = g_ref[e]
         value = jnp.dot(
             gstage[e].reshape(rows, outc), basis, preferred_element_type=f32
         ).astype(bf16)
@@ -199,22 +229,15 @@
             each(examples, lambda e: g_copy(q, j, 0, e, True).start())
         each(examples, lambda e: g_copy(q, 0, 1, e, True).start())
 
-    def own_project(e):
-        for q in range(HALVES):
-            project(q, f * examples + e)
-
-    each(examples, own_project)
-
-    def sibling_rotate(e):
-        x_arrival(0, 1, e).wait_recv()
-        rotate(sibling * examples + e)
-
-    each(examples, sibling_rotate)
+    each(examples, lambda e: project_whole(f * examples + e))
+
+    each(examples, lambda e: x_arrival(0, 1, e).wait_recv())
+    rotate([sibling * examples + e for e in range(examples)])
 
     def sibling_project(e):
         for q in range(HALVES):
             g_arrival(q, 0, 1, e).wait_recv()
-            project(q, sibling * examples + e)
+        project_whole(sibling * examples + e)
 
     each(examples, sibling_project)
 
@@ -222,9 +245,8 @@
         j, e = 1 + i // examples, i % examples
         x_arrival(j, 0, e).wait_recv()
         x_copy(j, 1, e, False).start()
-        rotate(source(j, 0) * examples + e)
         x_arrival(j, 1, e).wait_recv()
-        rotate(source(j, 1) * examples + e)
+        rotate([source(j, 0) * examples + e, source(j, 1) * examples + e])
 
     each((nh - 1) * examples, far_rotate)
 
@@ -298,15 +320,20 @@
     return pl.pallas_call(
         functools.partial(kernel, nd, nf, examples),
         out_shape=(out, out),
-        in_specs=[vmem] * 4,
+        in_specs=[pl.BlockSpec(memory_space=pl.ANY)] * 4,
         out_specs=(vmem, vmem),
         scratch_shapes=[
+            pltpu.VMEM(inputs.shape, bf16),
+            pltpu.VMEM(out_grads.shape, bf16),
+            pltpu.VMEM(patch_basis.shape, bf16),
+            pltpu.VMEM(output_basis.shape, bf16),
+            dma((4,)),
             pltpu.VMEM((held, side + 2, PADDED, channels), bf16),
             pltpu.VMEM((examples, side, PADDED, outc), bf16),
             pltpu.VMEM((nf, outc, own_cols), bf16),
             pltpu.VMEM((held, rows, cols), bf16),
             pltpu.VMEM((HALVES, held, rows, quart), bf16),
-            pltpu.VMEM((3 * (channels // LANES), (side + 2) * PADDED, LANES), bf16),
+            pltpu.VMEM((examples, 3 * (channels // LANES), (side + 2) * PADDED, LANES), bf16),
             pltpu.VMEM((2, (side + 2) * PADDED, (side + 2) * PADDED), bf16),
             pltpu.VMEM((HALVES, quart, cols), f32),
             pltpu.VMEM((HALVES, quart, cols), f32),

time: 54.8 us -> 53.4 us (0.974)
  Pallas kernels: 47.9 us -> 46.5 us
    pallas_call x1, Pallas kernels: 47.9 us -> 46.5 us  [on_device(): pl.pallas_call(functools.partial(kernel, nd, nf, examples), out_shape=(ou...]
where the time goes in v2:
time: 53.4 us; the launch traced here: 53.2 us
  Pallas kernels  46.5 us (87%)
  local copies, waits for them, and re-layouts  6.04 us (11%)
  between operations  0.67 us (1%)
    pallas_call x1, Pallas kernels, on_device(): pl.pallas_call(functools.partial(kernel, nd, nf, examples), out_shape=(ou...  46.5 us
    unnamed x8, local copies, waits for them, and re-layouts  6.04 us

profile of v2, /device:TPU:11, one launch (start us, length us, event | category | flops | bytes accessed | tf_op | source)
XLA Modules:
  0.0 53.2 jit_solution(1189559329594902863)
XLA Ops:
  0.6 0.0 copy-start
  0.6 1.0 %copy.9.ob_hbm = bf16[256,64]{1,0:T(8,128)(2,1)S(1)} copy(bf16[256,64]{0,1:T(8,128)(2,1)} %param.7) | data formatting | bytes 65536 | tf_op args[3]
  1.6 1.1 %copy.6.x_hbm = bf16[4,14,14,256]{3,2,1,0:T(8,128)(2,1)S(1)} copy(bf16[4,14,14,256]{3,0,2,1:T(4,128)(2,1)} %param.4) | data formatting | bytes 802816 | tf_op args[0]
  2.7 1.1 %copy.7.g_hbm = bf16[4,14,14,256]{3,2,1,0:T(8,128)(2,1)S(1)} copy(bf16[4,14,14,256]{3,0,2,1:T(4,128)(2,1)} %param.5) | data formatting | bytes 802816 | tf_op args[1]
  3.8 0.0 copy-done
  3.8 1.7 %copy.8.pb_hbm = bf16[1152,576]{1,0:T(8,128)(2,1)} copy(bf16[1152,576]{0,1:T(8,128)(2,1)S(1)} %copy-done) | data formatting | bytes 2654208 | tf_op args[2]
  5.4 46.5 %shard_map.59 = (f32[32,576]{1,0:T(8,128)S(1)}, f32[32,576]{1,0:T(8,128)S(1)}) custom-call(bf16[4,14,14,256]{3,2,1,0:T(8,128)(2,1)S(1)} %copy.6.x_hbm, bf16[4,14,14,256]{3,2,1,0:T(8,128)(2,1)S(1)} %copy.7.g_hbm, bf16[1152,576]{1,0:T(8,128)(2,1)} %copy.8.pb_hbm, bf16[256,64]{1,0:T(8,128)(2,1)S(1)} %copy.9.ob_hbm), custom_call_target="tpu_custom_call" | custom-call | tf_op jit(solution)/shard_map/pallas_call | solution.py:320
  51.9 0.6 %copy.12 = f32[32,576]{1,0:T(8,128)} copy(f32[32,576]{1,0:T(8,128)S(1)} %get-tuple-element.4) | data formatting | bytes 147456
  52.6 0.6 %copy.13 = f32[32,576]{1,0:T(8,128)} copy(f32[32,576]{1,0:T(8,128)S(1)} %get-tuple-element.5) | data formatting | bytes 147456
Async XLA Ops:
  0.6 3.1 %copy-start = (bf16[1152,576]{0,1:T(8,128)(2,1)S(1)}, bf16[1152,576]{0,1:T(8,128)(2,1)}, u32[]{:S(2)}) copy-start(bf16[1152,576]{0,1:T(8,128)(2,1)} %param.6) | copy-start | bytes 3981316

commit v3 on v2

--- a/solution.py
+++ b/solution.py
@@ -16,7 +16,7 @@
 
 def kernel(
     nd, nf, examples, x_hbm, g_hbm, pb_hbm, ob_hbm, sq_out, ln_out,
-    x_ref, g_ref, pb_ref, ob_ref, local,
+    x_ref, g_ref, pb_ref, ob_ref, local, basis_in,
     xbuf, gstage, obbuf, rot, gr, taps, shifts, sq, ln, rs_send, rs_recv,
     ob_snd, ob_rcv, x_snd, x_rcv, g_snd, g_rcv, r_snd, r_rcv,
 ):
@@ -27,9 +27,8 @@
     sibling = 2 * h + 1 - c
     side = x_ref.shape[1]
     channels = x_ref.shape[3]
-    height, cols = pb_ref.shape
-    outc = ob_ref.shape[0]
-    own_cols = ob_ref.shape[1]
+    cols, height = pb_ref.shape
+    own_cols, outc = ob_ref.shape
     rows = side * PADDED
     flat = xbuf.shape[1] * PADDED
     quart = outc // HALVES
@@ -143,8 +142,10 @@
     for j in range(1, nh):
         ob_copy(j, 0, True).start()
     ob_copy(0, 1, True).start()
-    for j in range(1, nh):
-        each(examples, lambda e: x_copy(j, 0, e, True).start())
+    first_in = examples // 2
+    for e in range(first_in):
+        for j in range(1, nh):
+            x_copy(j, 0, e, True).start()
     each(examples, lambda e: x_copy(0, 1, e, True).start())
 
     sq[...] = jnp.zeros_like(sq)
@@ -176,7 +177,7 @@
                 pieces.append(taps[b, kx * chunks + k, pl.ds(start, rows), :])
             lines.append(jnp.concatenate(pieces, axis=1))
         patches = jnp.concatenate(lines, axis=0)
-        value = jnp.dot(patches, pb_ref[...], preferred_element_type=f32).astype(bf16)
+        value = jnp.dot(patches, basis_in[...], preferred_element_type=f32).astype(bf16)
         for b, n in enumerate(slots):
             rot[n] = value[b * rows : (b + 1) * rows]
 
@@ -198,6 +199,7 @@
         ln[q] += value
 
     loads[3].wait()
+    basis_in[...] = pb_ref[...].T
     rotate([f * examples + e for e in range(examples)])
 
     ob_arrival(0, 1).wait_recv()
@@ -206,15 +208,15 @@
         ob_copy(j, 1, False).start()
     for j in range(1, nh):
         ob_arrival(j, 1).wait_recv()
-    column = lax.broadcasted_iota(jnp.int32, (own_cols, outc), 0)
-    place = lax.broadcasted_iota(jnp.int32, (own_cols, outc), 1)
+    column = lax.broadcasted_iota(jnp.int32, (outc, outc), 0)
+    place = lax.broadcasted_iota(jnp.int32, (outc, outc), 1)
     half, rest = place // quart, place % quart
     wanted = (rest // per_dp) * (per_dp * HALVES) + half * per_dp + rest % per_dp
-    basis = jnp.zeros((outc, outc), f32)
-    for s in range(nf):
-        pick = (column + s * own_cols == wanted).astype(f32).astype(bf16)
-        basis = basis + jnp.dot(obbuf[s], pick, preferred_element_type=f32)
-    basis = basis.astype(bf16)
+    pick = (column == wanted).astype(f32).astype(bf16)
+    basis = lax.dot_general(
+        obbuf[...].reshape(outc, outc), pick, (((0,), (0,)), ((), ())),
+        preferred_element_type=f32,
+    ).astype(bf16)
     loads[2].wait()
     for e in range(examples):
         gstage[e] = jnp.zeros((side, PADDED, outc), bf16)
@@ -225,21 +227,37 @@
         for q in range(HALVES):
             gr[q, f * examples + e] = value[:, q * quart : (q + 1) * quart]
     for q in range(HALVES):
+        each(examples, lambda e: g_copy(q, 0, 1, e, True).start())
+
+    def send_on(last, following):
         for j in range(1, nh):
-            each(examples, lambda e: g_copy(q, j, 0, e, True).start())
-        each(examples, lambda e: g_copy(q, 0, 1, e, True).start())
-
+            last(j).wait_send()
+            for later in following:
+                later(j).start()
+
+    for e in range(first_in):
+        send_on(
+            lambda j: x_copy(j, 0, e, True),
+            [lambda j: x_copy(j, 0, e + first_in, True)],
+        )
     each(examples, lambda e: project_whole(f * examples + e))
 
     each(examples, lambda e: x_arrival(0, 1, e).wait_recv())
     rotate([sibling * examples + e for e in range(examples)])
+
+    for e in range(first_in):
+        send_on(
+            lambda j: x_copy(j, 0, e + first_in, True),
+            [
+                lambda j: g_copy(0, j, 0, 2 * e, True),
+                lambda j: g_copy(0, j, 0, 2 * e + 1, True),
+            ],
+        )
 
     def sibling_project(e):
         for q in range(HALVES):
             g_arrival(q, 0, 1, e).wait_recv()
         project_whole(sibling * examples + e)
-
-    each(examples, sibling_project)
 
     def far_rotate(i):
         j, e = 1 + i // examples, i % examples
@@ -248,7 +266,10 @@
         x_arrival(j, 1, e).wait_recv()
         rotate([source(j, 0) * examples + e, source(j, 1) * examples + e])
 
-    each((nh - 1) * examples, far_rotate)
+    near = (nh - 1) * examples // 2
+    each(near, far_rotate)
+    each(examples, sibling_project)
+    each((nh - 1) * examples - near, lambda i: far_rotate(i + near))
 
     for q in range(HALVES):
         def far_project(i):
@@ -258,6 +279,9 @@
             project(q, source(j, 0) * examples + e)
             g_arrival(q, j, 1, e).wait_recv()
             project(q, source(j, 1) * examples + e)
+            if q + 1 < HALVES:
+                g_copy(q, j, 0, e, True).wait_send()
+                g_copy(q + 1, j, 0, e, True).start()
 
         each((nh - 1) * examples, far_project)
 
@@ -294,21 +318,21 @@
         ob_copy(j, 1, False).wait_send()
 
         def sent(e):
-            x_copy(j, 0, e, True).wait_send()
             x_copy(j, 1, e, False).wait_send()
+            g_copy(HALVES - 1, j, 0, e, True).wait_send()
             for q in range(HALVES):
-                g_copy(q, j, 0, e, True).wait_send()
                 g_copy(q, j, 1, e, False).wait_send()
 
         each(examples, sent)
 
 
 def on_device(inputs, out_grads, patch_basis, output_basis):
+    patch_basis, output_basis = patch_basis.T, output_basis.T
     nd, nf = lax.axis_size("dp"), lax.axis_size("fsdp")
     nh = nf // 2
     examples, side, _, channels = inputs.shape
-    cols = patch_basis.shape[1]
-    outc, own_cols = output_basis.shape
+    cols = patch_basis.shape[0]
+    own_cols, outc = output_basis.shape
     rows = side * PADDED
     quart = outc // HALVES
     per_dp = quart // nd
@@ -328,9 +352,10 @@
             pltpu.VMEM(patch_basis.shape, bf16),
             pltpu.VMEM(output_basis.shape, bf16),
             dma((4,)),
+            pltpu.VMEM(patch_basis.shape[::-1], bf16),
             pltpu.VMEM((held, side + 2, PADDED, channels), bf16),
             pltpu.VMEM((examples, side, PADDED, outc), bf16),
-            pltpu.VMEM((nf, outc, own_cols), bf16),
+            pltpu.VMEM((nf, own_cols, outc), bf16),
             pltpu.VMEM((held, rows, cols), bf16),
             pltpu.VMEM((HALVES, held, rows, quart), bf16),
             pltpu.VMEM((examples, 3 * (channels // LANES), (side + 2) * PADDED, LANES), bf16),

time: 53.4 us -> 51.6 us (0.966)
  local copies, waits for them, and re-layouts: 6.04 us -> 3.41 us
  Pallas kernels: 46.5 us -> 47.3 us
    unnamed x8 -> x6, local copies, waits for them, and re-layouts: 6.04 us -> 3.41 us
    pallas_call x1, Pallas kernels: 46.5 us -> 47.3 us  [on_device(): pl.pallas_call(functools.partial(kernel, nd, nf, examples), out_shape=(ou...]
where the time goes in v3:
time: 51.6 us; the launch traced here: 51.4 us
  Pallas kernels  47.3 us (92%)
  local copies, waits for them, and re-layouts  3.41 us (7%)
  between operations  0.66 us (1%)
    pallas_call x1, Pallas kernels, on_device(): pl.pallas_call(functools.partial(kernel, nd, nf, examples), out_shape=(ou...  47.3 us
    unnamed x6, local copies, waits for them, and re-layouts  3.41 us

profile of v3, /device:TPU:11, one launch (start us, length us, event | category | flops | bytes accessed | tf_op | source)
XLA Modules:
  0.0 51.4 jit_solution(15748388665668024693)
XLA Ops:
  0.6 0.0 copy-start
  0.6 1.1 %copy.6.x_hbm = bf16[4,14,14,256]{3,2,1,0:T(8,128)(2,1)S(1)} copy(bf16[4,14,14,256]{3,0,2,1:T(4,128)(2,1)} %param.4) | data formatting | bytes 802816 | tf_op args[0]
  1.7 1.1 %copy.7.g_hbm = bf16[4,14,14,256]{3,2,1,0:T(8,128)(2,1)S(1)} copy(bf16[4,14,14,256]{3,0,2,1:T(4,128)(2,1)} %param.5) | data formatting | bytes 802816 | tf_op args[1]
  2.8 0.0 copy-done
  2.8 47.3 %shard_map.59 = (f32[32,576]{1,0:T(8,128)S(1)}, f32[32,576]{1,0:T(8,128)S(1)}) custom-call(bf16[4,14,14,256]{3,2,1,0:T(8,128)(2,1)S(1)} %copy.6.x_hbm, bf16[4,14,14,256]{3,2,1,0:T(8,128)(2,1)S(1)} %copy.7.g_hbm, bf16[576,1152]{1,0:T(8,128)(2,1)} %bitcast.3, bf16[64,256]{1,0:T(8,128)(2,1)S(1)} %bitcast.2), custom_call_target="tpu_custom_call" | custom-call | tf_op jit(solution)/shard_map/pallas_call | solution.py:344
  50.1 0.6 %copy.10 = f32[32,576]{1,0:T(8,128)} copy(f32[32,576]{1,0:T(8,128)S(1)} %get-tuple-element.4) | data formatting | bytes 147456
  50.8 0.6 %copy.11 = f32[32,576]{1,0:T(8,128)} copy(f32[32,576]{1,0:T(8,128)S(1)} %get-tuple-element.5) | data formatting | bytes 147456
Async XLA Ops:
  0.6 2.1 %copy-start = (bf16[256,64]{0,1:T(8,128)(2,1)S(1)}, bf16[256,64]{0,1:T(8,128)(2,1)}, u32[]{:S(2)}) copy-start(bf16[256,64]{0,1:T(8,128)(2,1)} %param.7) | copy-start | bytes 98308

commit v4 on v3

--- a/solution.py
+++ b/solution.py
@@ -62,6 +62,9 @@
         xbuf[n, pl.ds(side + 1, xbuf.shape[1] - side - 1)] = jnp.zeros(
             (xbuf.shape[1] - side - 1, PADDED, channels), bf16
         )
+        rot[n, pl.ds(rows, flat - rows), :] = jnp.zeros((flat - rows, cols), bf16)
+        for q in range(HALVES):
+            gr[q, n, pl.ds(rows, flat - rows), :] = jnp.zeros((flat - rows, quart), bf16)
         return carry
 
     lax.fori_loop(0, nf * examples, clear, 0)
@@ -117,13 +120,13 @@
         to, back = route(j, t)
         s = f if own else source(j, 0)
         slot = back if t == 0 else j
-        ref = gr.at[q, s * examples + e]
+        ref = gr.at[q, s * examples + e, pl.ds(0, rows)]
         return pltpu.make_async_remote_copy(
             src_ref=ref, dst_ref=ref, send_sem=g_snd.at[q, j, t, e],
             recv_sem=g_rcv.at[q, slot, t, e], device_id=to, device_id_type=MESH)
 
     def g_arrival(q, j, t, e):
-        ref = gr.at[q, source(j, t) * examples + e]
+        ref = gr.at[q, source(j, t) * examples + e, pl.ds(0, rows)]
         return pltpu.make_async_remote_copy(
             src_ref=ref, dst_ref=ref, send_sem=g_snd.at[q, j, t, e],
             recv_sem=g_rcv.at[q, j, t, e], device_id=(d, sibling), device_id_type=MESH)
@@ -179,7 +182,7 @@
         patches = jnp.concatenate(lines, axis=0)
         value = jnp.dot(patches, basis_in[...], preferred_element_type=f32).astype(bf16)
         for b, n in enumerate(slots):
-            rot[n] = value[b * rows : (b + 1) * rows]
+            rot[n, pl.ds(0, rows), :] = value[b * rows : (b + 1) * rows]
 
     def project_whole(n):
         both = jnp.concatenate([gr[q, n] for q in range(HALVES)], axis=1)
@@ -200,88 +203,126 @@
 
     loads[3].wait()
     basis_in[...] = pb_ref[...].T
-    rotate([f * examples + e for e in range(examples)])
-
-    ob_arrival(0, 1).wait_recv()
-    for j in range(1, nh):
-        ob_arrival(j, 0).wait_recv()
-        ob_copy(j, 1, False).start()
-    for j in range(1, nh):
-        ob_arrival(j, 1).wait_recv()
-    column = lax.broadcasted_iota(jnp.int32, (outc, outc), 0)
-    place = lax.broadcasted_iota(jnp.int32, (outc, outc), 1)
-    half, rest = place // quart, place % quart
-    wanted = (rest // per_dp) * (per_dp * HALVES) + half * per_dp + rest % per_dp
-    pick = (column == wanted).astype(f32).astype(bf16)
-    basis = lax.dot_general(
-        obbuf[...].reshape(outc, outc), pick, (((0,), (0,)), ((), ())),
-        preferred_element_type=f32,
-    ).astype(bf16)
-    loads[2].wait()
-    for e in range(examples):
-        gstage[e] = jnp.zeros((side, PADDED, outc), bf16)
-        gstage[e, :, pl.ds(0, side), :] = g_ref[e]
-        value = jnp.dot(
-            gstage[e].reshape(rows, outc), basis, preferred_element_type=f32
-        ).astype(bf16)
-        for q in range(HALVES):
-            gr[q, f * examples + e] = value[:, q * quart : (q + 1) * quart]
-    for q in range(HALVES):
-        each(examples, lambda e: g_copy(q, 0, 1, e, True).start())
-
     def send_on(last, following):
         for j in range(1, nh):
             last(j).wait_send()
             for later in following:
                 later(j).start()
 
-    for e in range(first_in):
-        send_on(
-            lambda j: x_copy(j, 0, e, True),
-            [lambda j: x_copy(j, 0, e + first_in, True)],
-        )
-    each(examples, lambda e: project_whole(f * examples + e))
-
-    each(examples, lambda e: x_arrival(0, 1, e).wait_recv())
-    rotate([sibling * examples + e for e in range(examples)])
-
-    for e in range(first_in):
-        send_on(
-            lambda j: x_copy(j, 0, e + first_in, True),
-            [
-                lambda j: g_copy(0, j, 0, 2 * e, True),
-                lambda j: g_copy(0, j, 0, 2 * e + 1, True),
-            ],
-        )
-
-    def sibling_project(e):
-        for q in range(HALVES):
-            g_arrival(q, 0, 1, e).wait_recv()
-        project_whole(sibling * examples + e)
-
-    def far_rotate(i):
-        j, e = 1 + i // examples, i % examples
-        x_arrival(j, 0, e).wait_recv()
-        x_copy(j, 1, e, False).start()
-        x_arrival(j, 1, e).wait_recv()
-        rotate([source(j, 0) * examples + e, source(j, 1) * examples + e])
-
-    near = (nh - 1) * examples // 2
-    each(near, far_rotate)
-    each(examples, sibling_project)
-    each((nh - 1) * examples - near, lambda i: far_rotate(i + near))
-
-    for q in range(HALVES):
+    def rotate_gradients():
+        ob_arrival(0, 1).wait_recv()
+        for j in range(1, nh):
+            ob_arrival(j, 0).wait_recv()
+            ob_copy(j, 1, False).start()
+        for j in range(1, nh):
+            ob_arrival(j, 1).wait_recv()
+        column = lax.broadcasted_iota(jnp.int32, (outc, outc), 0)
+        place = lax.broadcasted_iota(jnp.int32, (outc, outc), 1)
+        half, rest = place // quart, place % quart
+        wanted = (rest // per_dp) * (per_dp * HALVES) + half * per_dp + rest % per_dp
+        pick = (column == wanted).astype(f32).astype(bf16)
+        basis = lax.dot_general(
+            obbuf[...].reshape(outc, outc), pick, (((0,), (0,)), ((), ())),
+            preferred_element_type=f32,
+        ).astype(bf16)
+        loads[2].wait()
+
+        def one(e):
+            gstage[e] = jnp.zeros((side, PADDED, outc), bf16)
+            gstage[e, :, pl.ds(0, side), :] = g_ref[e]
+            value = jnp.dot(
+                gstage[e].reshape(rows, outc), basis, preferred_element_type=f32
+            ).astype(bf16)
+            for q in range(HALVES):
+                gr[q, f * examples + e, pl.ds(0, rows), :] = value[:, q * quart : (q + 1) * quart]
+                g_copy(q, 0, 1, e, True).start()
+
+        each(examples, one)
+        for e in range(first_in):
+            send_on(
+                lambda j: x_copy(j, 0, e, True),
+                [lambda j: x_copy(j, 0, e + first_in, True)],
+            )
+
+    def queue_first_half():
+        for e in range(first_in):
+            send_on(
+                lambda j: x_copy(j, 0, e + first_in, True),
+                [
+                    lambda j: g_copy(0, j, 0, 2 * e, True),
+                    lambda j: g_copy(0, j, 0, 2 * e + 1, True),
+                ],
+            )
+
+    pairs = examples // 2
+
+    def pair(i):
+        @pl.when(i == pairs)
+        def _():
+            rotate_gradients()
+
+        k = i - examples
+        j, e = 1 + jnp.maximum(k, 0) // examples, jnp.maximum(k, 0) % examples
+
+        @pl.when((i >= pairs) & (i < examples))
+        def _():
+            for b in range(2):
+                x_arrival(0, 1, 2 * (i - pairs) + b).wait_recv()
+
+        @pl.when(i == examples)
+        def _():
+            queue_first_half()
+
+        @pl.when(i >= examples)
+        def _():
+            x_arrival(j, 0, e).wait_recv()
+            x_copy(j, 1, e, False).start()
+            x_arrival(j, 1, e).wait_recv()
+
+        near = jnp.where(i < pairs, f * examples + 2 * i, sibling * examples + 2 * (i - pairs))
+        n0 = jnp.where(i < examples, near, source(j, 0) * examples + e)
+        n1 = jnp.where(i < examples, near + 1, source(j, 1) * examples + e)
+        rotate([n0, n1])
+
+        @pl.when((i >= examples) & (i < 2 * examples))
+        def _():
+            def whole(b):
+                item = 2 * k + b
+                at = item % examples
+
+                @pl.when(item >= examples)
+                def _():
+                    for q in range(HALVES):
+                        g_arrival(q, 0, 1, at).wait_recv()
+
+                project_whole(jnp.where(item < examples, f, sibling) * examples + at)
+
+            each(2, whole)
+
+    each(examples + (nh - 1) * examples, pair)
+
+    def half_sum(q):
         def far_project(i):
             j, e = 1 + i // examples, i % examples
-            g_arrival(q, j, 0, e).wait_recv()
-            g_copy(q, j, 1, e, False).start()
-            project(q, source(j, 0) * examples + e)
-            g_arrival(q, j, 1, e).wait_recv()
-            project(q, source(j, 1) * examples + e)
-            if q + 1 < HALVES:
-                g_copy(q, j, 0, e, True).wait_send()
-                g_copy(q + 1, j, 0, e, True).start()
+
+            def one(t):
+                @pl.when(t == 0)
+                def _():
+                    g_arrival(q, j, 0, e).wait_recv()
+                    g_copy(q, j, 1, e, False).start()
+
+                    @pl.when(q + 1 < HALVES)
+                    def _():
+                        g_copy(q, j, 0, e, True).wait_send()
+                        g_copy(q + 1, j, 0, e, True).start()
+
+                @pl.when(t == 1)
+                def _():
+                    g_arrival(q, j, 1, e).wait_recv()
+
+                project(q, source(j, t) * examples + e)
+
+            each(2, one)
 
         each((nh - 1) * examples, far_project)
 
@@ -295,6 +336,8 @@
             r_copy(q, j).start()
 
         each(nd - 1, hand_out)
+
+    each(HALVES, half_sum)
 
     for q in range(HALVES):
         start = pl.multiple_of(d * per_dp, per_dp)
@@ -356,9 +399,9 @@
             pltpu.VMEM((held, side + 2, PADDED, channels), bf16),
             pltpu.VMEM((examples, side, PADDED, outc), bf16),
             pltpu.VMEM((nf, own_cols, outc), bf16),
-            pltpu.VMEM((held, rows, cols), bf16),
-            pltpu.VMEM((HALVES, held, rows, quart), bf16),
-            pltpu.VMEM((examples, 3 * (channels // LANES), (side + 2) * PADDED, LANES), bf16),
+            pltpu.VMEM((held, rows + 2 * PADDED, cols), bf16),
+            pltpu.VMEM((HALVES, held, rows + 2 * PADDED, quart), bf16),
+            pltpu.VMEM((2, 3 * (channels // LANES), (side + 2) * PADDED, LANES), bf16),
             pltpu.VMEM((2, (side + 2) * PADDED, (side + 2) * PADDED), bf16),
             pltpu.VMEM((HALVES, quart, cols), f32),
             pltpu.VMEM((HALVES, quart, cols), f32),

time: 51.6 us -> 53.5 us (1.037)
  Pallas kernels: 47.3 us -> 49 us
    pallas_call x1, Pallas kernels: 47.3 us -> 49 us  [on_device(): pl.pallas_call(functools.partial(kernel, nd, nf, examples), out_shape=(ou...]
where the time goes in v4:
time: 53.5 us; the launch traced here: 53 us
  Pallas kernels  49 us (92%)
  local copies, waits for them, and re-layouts  3.41 us (6%)
  between operations  0.66 us (1%)
    pallas_call x1, Pallas kernels, on_device(): pl.pallas_call(functools.partial(kernel, nd, nf, examples), out_shape=(ou...  49 us
    unnamed x6, local copies, waits for them, and re-layouts  3.41 us

profile of v4, /device:TPU:11, one launch (start us, length us, event | category | flops | bytes accessed | tf_op | source)
XLA Modules:
  0.0 53.0 jit_solution(10634548500083714598)
XLA Ops:
  0.6 0.0 copy-start
  0.6 1.1 %copy.6.x_hbm = bf16[4,14,14,256]{3,2,1,0:T(8,128)(2,1)S(1)} copy(bf16[4,14,14,256]{3,0,2,1:T(4,128)(2,1)} %param.4) | data formatting | bytes 802816 | tf_op args[0]
  1.7 1.1 %copy.7.g_hbm = bf16[4,14,14,256]{3,2,1,0:T(8,128)(2,1)S(1)} copy(bf16[4,14,14,256]{3,0,2,1:T(4,128)(2,1)} %param.5) | data formatting | bytes 802816 | tf_op args[1]
  2.8 0.0 copy-done
  2.8 49.0 %shard_map.59 = (f32[32,576]{1,0:T(8,128)S(1)}, f32[32,576]{1,0:T(8,128)S(1)}) custom-call(bf16[4,14,14,256]{3,2,1,0:T(8,128)(2,1)S(1)} %copy.6.x_hbm, bf16[4,14,14,256]{3,2,1,0:T(8,128)(2,1)S(1)} %copy.7.g_hbm, bf16[576,1152]{1,0:T(8,128)(2,1)} %bitcast.3, bf16[64,256]{1,0:T(8,128)(2,1)S(1)} %bitcast.2), custom_call_target="tpu_custom_call" | custom-call | tf_op jit(solution)/shard_map/pallas_call | solution.py:387
  51.8 0.6 %copy.10 = f32[32,576]{1,0:T(8,128)} copy(f32[32,576]{1,0:T(8,128)S(1)} %get-tuple-element.4) | data formatting | bytes 147456
  52.4 0.6 %copy.11 = f32[32,576]{1,0:T(8,128)} copy(f32[32,576]{1,0:T(8,128)S(1)} %get-tuple-element.5) | data formatting | bytes 147456
Async XLA Ops:
  0.6 2.1 %copy-start = (bf16[256,64]{0,1:T(8,128)(2,1)S(1)}, bf16[256,64]{0,1:T(8,128)(2,1)}, u32[]{:S(2)}) copy-start(bf16[256,64]{0,1:T(8,128)(2,1)} %param.7) | copy-start | bytes 98308

commit v5 on v3

--- a/solution.py
+++ b/solution.py
@@ -33,7 +33,6 @@
     flat = xbuf.shape[1] * PADDED
     quart = outc // HALVES
     per_dp = quart // nd
-    total = nd * nf * examples
     f32, bf16 = jnp.float32, jnp.bfloat16
 
     barrier = pltpu.get_barrier_semaphore()
@@ -142,10 +141,8 @@
     for j in range(1, nh):
         ob_copy(j, 0, True).start()
     ob_copy(0, 1, True).start()
-    first_in = examples // 2
-    for e in range(first_in):
-        for j in range(1, nh):
-            x_copy(j, 0, e, True).start()
+    for j in range(1, nh):
+        each(examples, lambda e: x_copy(j, 0, e, True).start())
     each(examples, lambda e: x_copy(0, 1, e, True).start())
 
     sq[...] = jnp.zeros_like(sq)
@@ -226,33 +223,15 @@
         ).astype(bf16)
         for q in range(HALVES):
             gr[q, f * examples + e] = value[:, q * quart : (q + 1) * quart]
+    for j in range(1, nh):
+        each(examples, lambda e: g_copy(0, j, 0, e, True).start())
     for q in range(HALVES):
         each(examples, lambda e: g_copy(q, 0, 1, e, True).start())
 
-    def send_on(last, following):
-        for j in range(1, nh):
-            last(j).wait_send()
-            for later in following:
-                later(j).start()
-
-    for e in range(first_in):
-        send_on(
-            lambda j: x_copy(j, 0, e, True),
-            [lambda j: x_copy(j, 0, e + first_in, True)],
-        )
     each(examples, lambda e: project_whole(f * examples + e))
 
     each(examples, lambda e: x_arrival(0, 1, e).wait_recv())
     rotate([sibling * examples + e for e in range(examples)])
-
-    for e in range(first_in):
-        send_on(
-            lambda j: x_copy(j, 0, e + first_in, True),
-            [
-                lambda j: g_copy(0, j, 0, 2 * e, True),
-                lambda j: g_copy(0, j, 0, 2 * e + 1, True),
-            ],
-        )
 
     def sibling_project(e):
         for q in range(HALVES):
@@ -305,8 +284,8 @@
             got = rs_recv[q, j].astype(f32)
             total_sq = total_sq + got[:per_dp]
             total_ln = total_ln + got[per_dp:]
-        sq_out[pl.ds(q * per_dp, per_dp), :] = total_sq * (1.0 / total)
-        ln_out[pl.ds(q * per_dp, per_dp), :] = total_ln * (1.0 / math.sqrt(total))
+        sq_out[pl.ds(q * per_dp, per_dp), :] = total_sq
+        ln_out[pl.ds(q * per_dp, per_dp), :] = total_ln
 
     ob_copy(0, 1, True).wait_send()
     each(examples, lambda e: x_copy(0, 1, e, True).wait_send())
@@ -318,6 +297,7 @@
         ob_copy(j, 1, False).wait_send()
 
         def sent(e):
+            x_copy(j, 0, e, True).wait_send()
             x_copy(j, 1, e, False).wait_send()
             g_copy(HALVES - 1, j, 0, e, True).wait_send()
             for q in range(HALVES):
@@ -341,7 +321,8 @@
     dma = pltpu.SemaphoreType.DMA
     vmem = pl.BlockSpec(memory_space=pltpu.VMEM)
     out = jax.ShapeDtypeStruct((outc // nd, cols), f32)
-    return pl.pallas_call(
+    total = nd * nf * examples
+    squares, linear = pl.pallas_call(
         functools.partial(kernel, nd, nf, examples),
         out_shape=(out, out),
         in_specs=[pl.BlockSpec(memory_space=pl.ANY)] * 4,
@@ -377,6 +358,7 @@
             collective_id=0, has_side_effects=True, vmem_limit_bytes=52 * 1024 * 1024
         ),
     )(inputs, out_grads, patch_basis, output_basis)
+    return squares * (1.0 / total), linear * (1.0 / math.sqrt(total))
 
 
 def solution(mesh):

time: 51.6 us -> 49.3 us (0.955)
  Pallas kernels: 47.3 us -> 45.7 us
  local copies, waits for them, and re-layouts: 3.41 us -> 2.13 us
  other arithmetic: 0 us -> 0.68 us
    pallas_call x1, Pallas kernels: 47.3 us -> 45.7 us  [on_device(): pl.pallas_call(functools.partial(kernel, nd, nf, examples), out_shape=(ou...]
    unnamed x6 -> x4, local copies, waits for them, and re-layouts: 3.41 us -> 2.13 us
    mul x0 -> x1, other arithmetic: none -> 0.68 us  [on_device(): return (squares * (1.0 / total), linear * (1.0 / math.sqrt(total)))]
where the time goes in v5:
time: 49.3 us; the launch traced here: 49.1 us
  Pallas kernels  45.7 us (93%)
  local copies, waits for them, and re-layouts  2.13 us (4%)
  other arithmetic  0.68 us (1%)
  between operations  0.66 us (1%)
    pallas_call x1, Pallas kernels, on_device(): pl.pallas_call(functools.partial(kernel, nd, nf, examples), out_shape=(ou...  45.7 us
    unnamed x4, local copies, waits for them, and re-layouts  2.13 us

profile of v5, /device:TPU:11, one launch (start us, length us, event | category | flops | bytes accessed | tf_op | source)
XLA Modules:
  0.0 49.1 jit_solution(17901052612907468624)
XLA Ops:
  0.6 0.0 copy-start
  0.6 1.1 %copy.6.x_hbm = bf16[4,14,14,256]{3,2,1,0:T(8,128)(2,1)S(1)} copy(bf16[4,14,14,256]{3,0,2,1:T(4,128)(2,1)} %param.4) | data formatting | bytes 802816 | tf_op args[0]
  1.7 1.1 %copy.7.g_hbm = bf16[4,14,14,256]{3,2,1,0:T(8,128)(2,1)S(1)} copy(bf16[4,14,14,256]{3,0,2,1:T(4,128)(2,1)} %param.5) | data formatting | bytes 802816 | tf_op args[1]
  2.8 0.0 copy-done
  2.8 45.7 %shard_map.59 = (f32[32,576]{1,0:T(8,128)S(1)}, f32[32,576]{1,0:T(8,128)S(1)}) custom-call(bf16[4,14,14,256]{3,2,1,0:T(8,128)(2,1)S(1)} %copy.6.x_hbm, bf16[4,14,14,256]{3,2,1,0:T(8,128)(2,1)S(1)} %copy.7.g_hbm, bf16[576,1152]{1,0:T(8,128)(2,1)} %bitcast.3, bf16[64,256]{1,0:T(8,128)(2,1)S(1)} %bitcast.2), custom_call_target="tpu_custom_call" | custom-call | tf_op jit(solution)/shard_map/pallas_call | solution.py:325
  48.5 0.7 %broadcast_multiply_fusion = (f32[32,576]{1,0:T(8,128)}, f32[32,576]{1,0:T(8,128)}) fusion(f32[32,576]{1,0:T(8,128)S(1)} %get-tuple-element.5, f32[32,576]{1,0:T(8,128)S(1)} %get-tuple-element.4), kind=kLoop, calls=%fused_computation | loop fusion | flops 36864 | bytes 294912 | tf_op jit(solution)/shard_map/mul | solution.py:361
Async XLA Ops:
  0.6 2.1 %copy-start = (bf16[256,64]{0,1:T(8,128)(2,1)S(1)}, bf16[256,64]{0,1:T(8,128)(2,1)}, u32[]{:S(2)}) copy-start(bf16[256,64]{0,1:T(8,128)(2,1)} %param.7) | copy-start | bytes 98308

commit v6 on v5

--- a/solution.py
+++ b/solution.py
@@ -223,9 +223,9 @@
         ).astype(bf16)
         for q in range(HALVES):
             gr[q, f * examples + e] = value[:, q * quart : (q + 1) * quart]
-    for j in range(1, nh):
-        each(examples, lambda e: g_copy(0, j, 0, e, True).start())
     for q in range(HALVES):
+        for j in range(1, nh):
+            each(examples, lambda e: g_copy(q, j, 0, e, True).start())
         each(examples, lambda e: g_copy(q, 0, 1, e, True).start())
 
     each(examples, lambda e: project_whole(f * examples + e))
@@ -258,9 +258,6 @@
             project(q, source(j, 0) * examples + e)
             g_arrival(q, j, 1, e).wait_recv()
             project(q, source(j, 1) * examples + e)
-            if q + 1 < HALVES:
-                g_copy(q, j, 0, e, True).wait_send()
-                g_copy(q + 1, j, 0, e, True).start()
 
         each((nh - 1) * examples, far_project)
 
@@ -299,8 +296,8 @@
         def sent(e):
             x_copy(j, 0, e, True).wait_send()
             x_copy(j, 1, e, False).wait_send()
-            g_copy(HALVES - 1, j, 0, e, True).wait_send()
             for q in range(HALVES):
+                g_copy(q, j, 0, e, True).wait_send()
                 g_copy(q, j, 1, e, False).wait_send()
 
         each(examples, sent)

time: 49.3 us -> 49.3 us (level)
  no operation moved by 1% of the time
where the time goes in v6:
time: 49.3 us; the launch traced here: 49.1 us
  Pallas kernels  45.7 us (93%)
  local copies, waits for them, and re-layouts  2.13 us (4%)
  other arithmetic  0.68 us (1%)
  between operations  0.66 us (1%)
    pallas_call x1, Pallas kernels, on_device(): pl.pallas_call(functools.partial(kernel, nd, nf, examples), out_shape=(ou...  45.7 us
    unnamed x4, local copies, waits for them, and re-layouts  2.13 us

profile of v6, /device:TPU:11, one launch (start us, length us, event | category | flops | bytes accessed | tf_op | source)
XLA Modules:
  0.0 49.1 jit_solution(9668247536802961489)
XLA Ops:
  0.6 0.0 copy-start
  0.6 1.1 %copy.6.x_hbm = bf16[4,14,14,256]{3,2,1,0:T(8,128)(2,1)S(1)} copy(bf16[4,14,14,256]{3,0,2,1:T(4,128)(2,1)} %param.4) | data formatting | bytes 802816 | tf_op args[0]
  1.7 1.1 %copy.7.g_hbm = bf16[4,14,14,256]{3,2,1,0:T(8,128)(2,1)S(1)} copy(bf16[4,14,14,256]{3,0,2,1:T(4,128)(2,1)} %param.5) | data formatting | bytes 802816 | tf_op args[1]
  2.8 0.0 copy-done
  2.8 45.7 %shard_map.59 = (f32[32,576]{1,0:T(8,128)S(1)}, f32[32,576]{1,0:T(8,128)S(1)}) custom-call(bf16[4,14,14,256]{3,2,1,0:T(8,128)(2,1)S(1)} %copy.6.x_hbm, bf16[4,14,14,256]{3,2,1,0:T(8,128)(2,1)S(1)} %copy.7.g_hbm, bf16[576,1152]{1,0:T(8,128)(2,1)} %bitcast.3, bf16[64,256]{1,0:T(8,128)(2,1)S(1)} %bitcast.2), custom_call_target="tpu_custom_call" | custom-call | tf_op jit(solution)/shard_map/pallas_call | solution.py:322
  48.5 0.7 %broadcast_multiply_fusion = (f32[32,576]{1,0:T(8,128)}, f32[32,576]{1,0:T(8,128)}) fusion(f32[32,576]{1,0:T(8,128)S(1)} %get-tuple-element.5, f32[32,576]{1,0:T(8,128)S(1)} %get-tuple-element.4), kind=kLoop, calls=%fused_computation | loop fusion | flops 36864 | bytes 294912 | tf_op jit(solution)/shard_map/mul | solution.py:358
Async XLA Ops:
  0.6 2.1 %copy-start = (bf16[256,64]{0,1:T(8,128)(2,1)S(1)}, bf16[256,64]{0,1:T(8,128)(2,1)}, u32[]{:S(2)}) copy-start(bf16[256,64]{0,1:T(8,128)(2,1)} %param.7) | copy-start | bytes 98308
